TPU v7x, 128 devices: a whole 4x4x4 slice. The times are simulated.
128 devices in a mesh: row: 16 (over y, x_hi, core), col: 8 (over z, x_lo).
Axes of the slice: x: 4 (x_hi: 2, x_lo: 2; x = x_hi * 2 + x_lo), y: 4, z: 4, core: 2. Of those that a mesh axis runs over, the one named last changes fastest.
Arguments:
- a_blocks: bfloat16 [128, 256, 128, 128], P('row', 'col'), may hold values from -6 to 6
- a_pattern: int32 [128, 256], P('row', 'col'), may hold values from 0 to 1, as said below
- b_blocks: bfloat16 [256, 128, 128, 128], P('row', 'col'), may hold values from -0.5 to 0.5
- b_pattern: int32 [256, 128], P('row', 'col'), may hold values from 0 to 1, as said below
Outputs:
- c_blocks: float32 [128, 128, 128, 128], P('row', 'col')
Inputs may be any that keep to these rules, and one draw needn't show every extreme that they name: `a_pattern`: each tile of 8 x 16 entries holds at most 16 ones, and in every tile row one tile holds exactly 16. `b_pattern`: each tile of 16 x 8 entries holds at most 16 ones, and in every tile row one tile holds exactly 16.
All inputs are finite; a program needn't handle non-finite values.
Results may differ from a plain program's by a relative error of at most 0.0003.
Values may be sent and summed in bfloat16 or wider, within the bound.
No kernel may reach another device: no remote copies, remote signals or barrier semaphores. Data moves between devices by JAX's collectives and lax.ppermute only.
A program may use at most 128 MiB of HBM per device.

v0:
```python
import jax
import jax.numpy as jnp
from jax import lax
from jax.sharding import PartitionSpec as P


def passed_along(value, axis, steps):
    count = lax.axis_size(axis)
    pairs = [(source, (source + steps) % count) for source in range(count)]
    return lax.ppermute(value, axis, pairs)


def masked(blocks, pattern):
    return blocks * pattern[:, :, None, None].astype(blocks.dtype)


def tile_product(left_blocks, right_blocks, tile_count):
    row_count = left_blocks.shape[0]
    inner_count = left_blocks.shape[1] // tile_count
    col_count = right_blocks.shape[1] // tile_count
    block_size = left_blocks.shape[2]
    left_tiles = left_blocks.reshape(row_count, tile_count, inner_count, block_size, block_size)
    right_tiles = right_blocks.reshape(inner_count, tile_count, col_count, block_size, block_size)
    product = jnp.einsum(
        "atkxy,ktcyz->atcxz", left_tiles, right_tiles, preferred_element_type=jnp.float32
    )
    return product.reshape(row_count, tile_count * col_count, block_size, block_size)


def shards(a_blocks, a_pattern, b_blocks, b_pattern):
    tile_count = lax.axis_size("row") // lax.axis_size("col")
    inner_count = a_blocks.shape[1] // tile_count
    a_here = masked(a_blocks, a_pattern)
    b_here = masked(b_blocks, b_pattern)
    first_sum = tile_product(a_here, b_here, tile_count)
    a_marks = a_pattern.astype(jnp.bfloat16)
    moved_tile, moved_marks = passed_along(
        (a_here[:, :inner_count], a_marks[:, :inner_count]), "col", -1
    )
    b_later = passed_along(b_here, "row", -1)
    a_later = jnp.concatenate([a_here[:, inner_count:], moved_tile], axis=1)
    second_sum = tile_product(a_later, b_later, tile_count)
    return first_sum + second_sum


def solution(mesh):
    return jax.shard_map(
        shards,
        mesh=mesh,
        in_specs=(
            P("row", "col", None, None),
            P("row", "col"),
            P("row", "col", None, None),
            P("row", "col"),
        ),
        out_specs=P("row", "col", None, None),
        check_vma=False,
    )
```

profile of v0, /device:TPU:0, one launch (start us, length us, event | category | flops | bytes accessed | tf_op | source)
XLA Modules:
  0.0 239.7 jit_solution(6865793015322386815)
XLA Ops:
  0.0 0.7 convert_element_type.8
  0.7 0.0 copy-start.1
  0.7 7.2 %broadcast_multiply_fusion.1 = bf16[16,16,128,128]{3,2,1,0:T(8,128)(2,1)} fusion(bf16[16,16,128,128]{3,2,1,0:T(8,128)(2,1)} %param.6, bf16[16,16]{1,0:T(8,128)(2,1)S(1)} %convert_element_type.8), kind=kLoop, calls=%fused_computation.8 | loop fusion | flops 4194304 | bytes 16777728 | tf_op jit(solution)/shard_map/mul | solution.py:14
  7.9 5.0 %collective-permute-start = (bf16[16,16,128,128]{3,2,1,0:T(8,128)(2,1)}, bf16[16,16,128,128]{3,2,1,0:T(8,128)(2,1)}, u32[]{:S(2)}, u32[]{:S(2)}) collective-permute-start(bf16[16,16,128,128]{3,2,1,0:T(8,128)(2,1)} %broadcast_multiply_fusion.1), channel_id=1, source_target_pairs={{0,120},{8,0},{16,8},{24,16},{32,24},{40,32},{48,40},{56,48},{64,5... | collective-permute-start | bytes 25165832 | tf_op jit(solution)/shard_map/ppermute | solution.py:10
  12.9 0.0 copy-done.1
  12.9 7.4 %broadcast_multiply_fusion = bf16[8,32,128,128]{3,2,1,0:T(8,128)(2,1)} fusion(bf16[8,32,128,128]{3,2,1,0:T(8,128)(2,1)} %param.4, bf16[8,32]{1,0:T(8,128)(2,1)S(1)} %convert_element_type.9), kind=kLoop, calls=%fused_computation.7 | loop fusion | flops 4194304 | bytes 16777728 | tf_op jit(solution)/shard_map/mul | solution.py:14
  20.3 0.0 copy-start
  20.3 5.4 %fusion.7 = (bf16[8,16,128,128]{3,2,1,0:T(8,128)(2,1)}, bf16[8,16,128,128]{3,2,1,0:T(8,128)(2,1)S(1)}) fusion(bf16[8,32,128,128]{3,2,1,0:T(8,128)(2,1)} %broadcast_multiply_fusion), kind=kLoop, calls=%fused_computation.9 | loop fusion | bytes 16777216 | tf_op jit(solution)/shard_map/slice | solution.py:41
  25.7 4.1 %collective-permute-start.1 = (bf16[8,16,128,128]{3,2,1,0:T(8,128)(2,1)S(1)}, bf16[8,16,128,128]{3,2,1,0:T(8,128)(2,1)}, u32[]{:S(2)}, u32[]{:S(2)}) collective-permute-start(bf16[8,16,128,128]{3,2,1,0:T(8,128)(2,1)S(1)} %get-tuple-element.6), channel_id=1, source_target_pairs={{0,7},{1,0},{2,1},{3,2},{4,3},{5,4},{6,5},{7,6},{8,15},{9,8},{10,9... | collective-permute-start | bytes 12582920 | tf_op jit(solution)/shard_map/ppermute | solution.py:10
  29.8 0.0 copy-done
  29.8 14.6 %fusion.2 = f32[2,8,128,8,128,1]{4,2,5,3,1,0:T(8,128)} fusion(bf16[8,2,16,128,128,1]{4,3,2,1,0,5:T(8,128)(2,1)S(1)} %bitcast.24, bf16[16,2,8,128,128,1]{4,3,2,1,0,5:T(8,128)(2,1)} %bitcast.25), kind=kOutput, calls=%fused_computation.4 | convolution fusion | flops 8589934592 | bytes 25165824 | tf_op jit(solution)/shard_map/atkxy,ktcyz->atcxz/dot_general | solution.py:24
  44.4 150.7 %collective-permute-done.1 = bf16[8,16,128,128]{3,2,1,0:T(8,128)(2,1)} collective-permute-done((bf16[8,16,128,128]{3,2,1,0:T(8,128)(2,1)S(1)}, bf16[8,16,128,128]{3,2,1,0:T(8,128)(2,1)}, u32[]{:S(2)}, u32[]{:S(2)}) %collective-permute-start.1) | collective-permute-done | bytes 4194336 | tf_op jit(solution)/shard_map/ppermute | solution.py:10
  195.1 7.4 %pad_maximum_fusion = bf16[8,32,128,128]{3,2,1,0:T(8,128)(2,1)} fusion(bf16[8,16,128,128]{3,2,1,0:T(8,128)(2,1)} %collective-permute-done.1, bf16[8,16,128,128]{3,2,1,0:T(8,128)(2,1)} %get-tuple-element.5), kind=kLoop, calls=%fused_computation | loop fusion | flops 4194304 | bytes 16777216 | tf_op jit(solution)/shard_map/concatenate | solution.py:41
  202.5 0.0 collective-permute-done
  202.5 12.3 %copy.11 = bf16[16,16,128,128]{2,3,0,1:T(8,128)(2,1)} copy(bf16[16,16,128,128]{3,2,1,0:T(8,128)(2,1)} %collective-permute-done) | data formatting | bytes 16777216 | tf_op jit(solution)/shard_map/ppermute | solution.py:10
  214.9 15.7 %bitcast_add_fusion = f32[2,8,128,8,128]{4,2,3,1,0:T(8,128)} fusion(f32[2,8,128,8,128,1]{4,2,5,3,1,0:T(8,128)} %fusion.2, bf16[16,2,8,128,128,1]{3,4,0,5,2,1:T(8,128)(2,1)} %bitcast.27, bf16[8,2,16,128,128,1]{4,3,2,1,0,5:T(8,128)(2,1)} %bitcast.26), kind=kOutput, calls=%fused_computation.1 | convolution fusion | flops 8592031744 | bytes 33554432 | tf_op jit(solution)/shard_map/atkxy,ktcyz->atcxz/dot_general | solution.py:24
  230.6 9.1 %copy.13 = f32[8,16,128,128]{3,2,1,0:T(8,128)} copy(f32[8,16,128,128]{2,3,0,1:T(8,128)} %bitcast.28) | data formatting | bytes 16777216 | tf_op jit(solution)/shard_map/add | solution.py:43
  (1 shorter events, 0.0 us)
Async XLA Ops:
  0.7 12.2 %copy-start.1 = (s32[8,32]{1,0:T(8,128)S(1)}, s32[8,32]{1,0:T(8,128)}, u32[]{:S(2)}) copy-start(s32[8,32]{1,0:T(8,128)} %param.5) | copy-start | bytes 3076
  7.9 194.6 %collective-permute-start = (bf16[16,16,128,128]{3,2,1,0:T(8,128)(2,1)}, bf16[16,16,128,128]{3,2,1,0:T(8,128)(2,1)}, u32[]{:S(2)}, u32[]{:S(2)}) collective-permute-start(bf16[16,16,128,128]{3,2,1,0:T(8,128)(2,1)} %broadcast_multiply_fusion.1), channel_id=1, source_target_pairs={{0,120},{8,0},{16,8},{24,16},{32,24},{40,32},{48,40},{56,48},{64,5... | collective-permute-start | bytes 25165832 | tf_op jit(solution)/shard_map/ppermute | solution.py:10
  20.3 9.4 %copy-start = (bf16[8,32,128,128]{3,2,1,0:T(8,128)(2,1)S(1)}, bf16[8,32,128,128]{3,2,1,0:T(8,128)(2,1)}, u32[]{:S(2)}) copy-start(bf16[8,32,128,128]{3,2,1,0:T(8,128)(2,1)} %broadcast_multiply_fusion) | copy-start | bytes 25165828
  25.7 169.4 %collective-permute-start.1 = (bf16[8,16,128,128]{3,2,1,0:T(8,128)(2,1)S(1)}, bf16[8,16,128,128]{3,2,1,0:T(8,128)(2,1)}, u32[]{:S(2)}, u32[]{:S(2)}) collective-permute-start(bf16[8,16,128,128]{3,2,1,0:T(8,128)(2,1)S(1)} %get-tuple-element.6), channel_id=1, source_target_pairs={{0,7},{1,0},{2,1},{3,2},{4,3},{5,4},{6,5},{7,6},{8,15},{9,8},{10,9... | collective-permute-start | bytes 12582920 | tf_op jit(solution)/shard_map/ppermute | solution.py:10
where the time goes:
time: 242 us; the launch traced here: 240 us
  waiting for transfers between devices  151 us (62%)
  matrix products  30.3 us (13%)
  local copies, waits for them, and re-layouts  26.8 us (11%)
  other arithmetic  22.7 us (9%)
  starting transfers between devices  9.06 us (4%)
    ppermute x2, waiting for transfers between devices, passed_along(): return lax.ppermute(value, axis, pairs)  151 us
    dot_general x2, matrix products, tile_product(): jnp.einsum('atkxy,ktcyz->atcxz', left_tiles, right_tiles, preferred_eleme...  30.3 us
    mul x2, other arithmetic, masked(): return blocks * pattern[:, :, None, None].astype(blocks.dtype)  14.6 us
    ppermute x1, local copies, waits for them, and re-layouts, passed_along(): return lax.ppermute(value, axis, pairs)  12.3 us
    add x1, local copies, waits for them, and re-layouts, shards(): return first_sum + second_sum  9.13 us
    ppermute x2, starting transfers between devices, passed_along(): return lax.ppermute(value, axis, pairs)  9.06 us
    concatenate x1, other arithmetic, shards(): a_later = jnp.concatenate([a_here[:, inner_count:], moved_tile], axis=1)  7.4 us
    slice x1, local copies, waits for them, and re-layouts, shards(): a_later = jnp.concatenate([a_here[:, inner_count:], moved_tile], axis=1)  5.37 us
  transfers between devices with their start and end apart: 2, of which 1 were waited for; matrix products, arithmetic and copies ran while one was open for 15% of the time, Pallas kernels for 0%

commit v1 on v0

v1 whole, which is shorter than its diff:
```python
import functools

import jax
import jax.numpy as jnp
from jax import lax
from jax.experimental import pallas as pl
from jax.experimental.pallas import tpu as pltpu
from jax.sharding import PartitionSpec as P

BR, KS, BC = 8, 16, 8
CAP = 16
BLOCK = 128
UNROLL = 4
PAIRS, TOUCHED, LIST = 8, 160, 256
ANY = pl.BlockSpec(memory_space=pl.ANY)
HBM = pl.BlockSpec(memory_space=pltpu.HBM)
SMEM = pl.BlockSpec(memory_space=pltpu.SMEM)


def passed_along(value, axis, steps):
    count = lax.axis_size(axis)
    pairs = [(source, (source + steps) % count) for source in range(count)]
    return lax.ppermute(value, axis, pairs)


def present(pattern, first_col, rows, cols, places, starts=None):
    count = jnp.int32(0)
    for row in range(rows):
        if starts is not None:
            starts[row] = count
        for col in range(cols):
            places[count] = row * cols + col
            count = count + pattern[row, first_col + col]
    if starts is not None:
        starts[rows] = count
    return count


def gather(pattern, first_col, rows, cols, source, packed, places, sem):
    count = present(pattern, first_col, rows, cols, places)

    def start(slot, carry):
        place = places[slot]
        pltpu.make_async_copy(
            source.at[place // cols, first_col + place % cols], packed.at[slot], sem
        ).start()
        return carry

    lax.fori_loop(0, count, start, 0)
    return count


def drain(count, source, target, sem):
    def wait(_, carry):
        pltpu.make_async_copy(source, target, sem).wait()
        return carry

    lax.fori_loop(0, count, wait, 0)


def pack_kernel(rows, cols, pattern, blocks, _, packed_0, packed_1, places_0, places_1, sem):
    count = gather(pattern, 0, rows, cols, blocks, packed_0, places_0, sem)
    count += gather(pattern, cols, rows, cols, blocks, packed_1, places_1, sem)
    drain(count, blocks.at[0, 0], packed_0.at[0], sem)


def pack(blocks, pattern, rows, cols, after):
    slots = pltpu.VMEM((CAP, BLOCK, BLOCK), blocks.dtype)
    return pl.pallas_call(
        functools.partial(pack_kernel, rows, cols),
        out_shape=(slots, slots),
        in_specs=[SMEM, HBM, ANY],
        out_specs=(ANY, ANY),
        scratch_shapes=[
            pltpu.SMEM((CAP + 1,), jnp.int32),
            pltpu.SMEM((CAP + 1,), jnp.int32),
            pltpu.SemaphoreType.DMA,
        ],
        compiler_params=pltpu.CompilerParams(vmem_limit_bytes=56 * 2**20),
        name="pack",
    )(pattern, blocks, after)


def list_pairs(a_pattern, a_col, b_pattern, b_col, out, a_places, b_places, b_starts, seen):
    a_count = present(a_pattern, a_col, BR, KS, a_places)
    present(b_pattern, b_col, KS, BC, b_places, b_starts)
    for place in range(BR * BC):
        seen[place] = 0

    def over_a(a_slot, counts):
        place = a_places[a_slot]
        row, inner = place // KS, place % KS

        def over_b(b_slot, counts):
            pairs, touched = counts
            target = row * BC + b_places[b_slot] % BC
            out[PAIRS + pairs] = a_slot + b_slot * 256 + target * 65536
            out[TOUCHED + touched] = target
            touched = touched + 1 - seen[target]
            seen[target] = 1
            return pairs + 1, touched

        return lax.fori_loop(b_starts[inner], b_starts[inner + 1], over_b, counts)

    pairs, touched = lax.fori_loop(0, a_count, over_a, (jnp.int32(0), jnp.int32(0)))
    for extra in range(UNROLL - 1):
        out[PAIRS + pairs + extra] = BR * BC * 65536
    out[0] = (pairs + UNROLL - 1) // UNROLL
    out[1] = touched


def multiply(pairs, a_slots, b_slots, total, first_col):
    def step(index, carry):
        products = []
        for part in range(UNROLL):
            pair = pairs[PAIRS + index * UNROLL + part]
            a_slot, b_slot, target = pair % 256, (pair // 256) % 256, pair // 65536
            product = jnp.dot(a_slots[a_slot], b_slots[b_slot], preferred_element_type=jnp.float32)
            products.append((target // BC, first_col + target % BC, product))
        for row, col, product in products:
            total[row, col] += product
        return carry

    lax.fori_loop(0, pairs[0], step, 0)


LIST_SCRATCH = [
    pltpu.SMEM((CAP + 1,), jnp.int32),
    pltpu.SMEM((CAP + 1,), jnp.int32),
    pltpu.SMEM((KS + 1,), jnp.int32),
    pltpu.SMEM((BR * BC,), jnp.int32),
]


def later_lists_kernel(a_pattern, a_next, b_next, list_0, list_1, *scratch):
    list_pairs(a_pattern, KS, b_next, 0, list_0, *scratch)
    list_pairs(a_next, 0, b_next, BC, list_1, *scratch)


def later_lists(a_pattern, a_next, b_next):
    lists = jax.ShapeDtypeStruct((LIST,), jnp.int32)
    return pl.pallas_call(
        later_lists_kernel,
        out_shape=(lists, lists),
        in_specs=[SMEM] * 3,
        out_specs=(SMEM, SMEM),
        scratch_shapes=LIST_SCRATCH,
        name="later_lists",
    )(a_pattern, a_next, b_next)


def first_kernel(
    a_pattern, b_pattern, a_0, a_1, b_0, b_1, result,
    total, a_held, b_held, own_0, own_1, sems, *scratch,
):
    loads = [
        pltpu.make_async_copy(packed, held, sems.at[index])
        for index, (packed, held) in enumerate(
            [(a_0, a_held.at[0]), (b_0, b_held.at[0]), (a_1, a_held.at[1]), (b_1, b_held.at[1])]
        )
    ]
    for load in loads:
        load.start()

    def clear(row, carry):
        total[row] = jnp.zeros(total.shape[1:], total.dtype)
        return carry

    lax.fori_loop(0, BR, clear, 0)
    list_pairs(a_pattern, 0, b_pattern, 0, own_0, *scratch)
    list_pairs(a_pattern, KS, b_pattern, BC, own_1, *scratch)
    for load in loads:
        load.wait()
    multiply(own_0, a_held.at[0], b_held.at[0], total, 0)
    multiply(own_1, a_held.at[1], b_held.at[1], total, BC)
    store = pltpu.make_async_copy(total.at[pl.ds(0, BR)], result, sems.at[4])
    store.start()
    store.wait()


def first(a_pattern, b_pattern, a_0, a_1, b_0, b_1):
    return pl.pallas_call(
        first_kernel,
        out_shape=jax.ShapeDtypeStruct((BR, 2 * BC, BLOCK, BLOCK), jnp.float32),
        in_specs=[SMEM] * 2 + [ANY] * 4,
        out_specs=ANY,
        scratch_shapes=[
            pltpu.VMEM((BR + 1, 2 * BC, BLOCK, BLOCK), jnp.float32),
            pltpu.VMEM((2, CAP, BLOCK, BLOCK), jnp.bfloat16),
            pltpu.VMEM((2, CAP, BLOCK, BLOCK), jnp.bfloat16),
            pltpu.SMEM((LIST,), jnp.int32),
            pltpu.SMEM((LIST,), jnp.int32),
            pltpu.SemaphoreType.DMA((5,)),
            *LIST_SCRATCH,
        ],
        compiler_params=pltpu.CompilerParams(vmem_limit_bytes=24 * 2**20),
        cost_estimate=pl.CostEstimate(flops=0, bytes_accessed=20 * 2**20, transcendentals=0),
        name="first_product",
    )(a_pattern, b_pattern, a_0, a_1, b_0, b_1)


def add_kernel(first_col, pairs, a_slots, b_slots, _, result, total, a_held, b_held, sems):
    load_a = pltpu.make_async_copy(a_slots, a_held, sems.at[0])
    load_b = pltpu.make_async_copy(b_slots, b_held, sems.at[1])
    load_a.start()
    load_b.start()
    touched = pairs[1]

    def block(index):
        target = pairs[TOUCHED + index]
        row, col = target // BC, target % BC
        return result.at[row, first_col + col], total.at[row, col]

    def load(index, carry):
        there, here = block(index)
        pltpu.make_async_copy(there, here, sems.at[2]).start()
        return carry

    def store(index, carry):
        there, here = block(index)
        pltpu.make_async_copy(here, there, sems.at[3]).start()
        return carry

    lax.fori_loop(0, touched, load, 0)
    load_a.wait()
    load_b.wait()
    drain(touched, result.at[0, 0], total.at[0, 0], sems.at[2])
    multiply(pairs, a_held, b_held, total, 0)
    lax.fori_loop(0, touched, store, 0)
    drain(touched, total.at[0, 0], result.at[0, 0], sems.at[3])


def add(pairs, a_slots, b_slots, result, first_col):
    return pl.pallas_call(
        functools.partial(add_kernel, first_col),
        out_shape=jax.ShapeDtypeStruct(result.shape, result.dtype),
        in_specs=[SMEM, ANY, ANY, ANY],
        out_specs=ANY,
        scratch_shapes=[
            pltpu.VMEM((BR + 1, BC, BLOCK, BLOCK), jnp.float32),
            pltpu.VMEM((CAP, BLOCK, BLOCK), jnp.bfloat16),
            pltpu.VMEM((CAP, BLOCK, BLOCK), jnp.bfloat16),
            pltpu.SemaphoreType.DMA((4,)),
        ],
        input_output_aliases={3: 0},
        compiler_params=pltpu.CompilerParams(vmem_limit_bytes=16 * 2**20),
        name="second_product",
    )(pairs, a_slots, b_slots, result)


def shards(a_blocks, a_pattern, b_blocks, b_pattern):
    a_next = passed_along(a_pattern, "col", -1)
    b_next = passed_along(b_pattern, "row", -1)
    b_0, b_1 = pack(b_blocks, b_pattern, KS, BC, b_pattern)
    b_later_0 = passed_along(b_0, "row", -1)
    b_later_1 = passed_along(b_1, "row", -1)
    list_0, list_1 = later_lists(a_pattern, a_next, b_next)
    a_0, a_1 = pack(a_blocks, a_pattern, BR, KS, list_0)
    a_later = passed_along(a_0, "col", -1)
    result = first(a_pattern, b_pattern, a_0, a_1, b_0, b_1)
    result = add(list_0, a_1, b_later_0, result, 0)
    return add(list_1, a_later, b_later_1, result, BC)


def solution(mesh):
    return jax.shard_map(
        shards,
        mesh=mesh,
        in_specs=(
            P("row", "col", None, None),
            P("row", "col"),
            P("row", "col", None, None),
            P("row", "col"),
        ),
        out_specs=P("row", "col", None, None),
        check_vma=False,
    )
```

time: 242 us -> 39 us (0.16)
  waiting for transfers between devices: 151 us -> 8.01 us
  matrix products: 30.3 us -> 0 us
  local copies, waits for them, and re-layouts: 26.8 us -> 1.19 us
  other arithmetic: 22.7 us -> 0 us
  Pallas kernels: 0 us -> 18.4 us
    ppermute x2 -> x5, waiting for transfers between devices: 151 us -> 8.01 us  [passed_along(): return lax.ppermute(value, axis, pairs)]
    dot_general x2 -> x0, matrix products: 30.3 us -> none  [tile_product(): jnp.einsum('atkxy,ktcyz->atcxz', left_tiles, right_tiles, preferred_eleme...]
    pallas_call x0 -> x6, Pallas kernels: none -> 18.4 us  [the longest x1 6.66 us: first(): pl.pallas_call(first_kernel, out_shape=jax.ShapeDtypeStruct((BR, 2 * BC,...]
    mul x2 -> x0, other arithmetic: 14.6 us -> none  [masked(): return blocks * pattern[:, :, None, None].astype(blocks.dtype)]
    ppermute x1 -> x0, local copies, waits for them, and re-layouts: 12.3 us -> none  [passed_along(): return lax.ppermute(value, axis, pairs)]
    add x1 -> x0, local copies, waits for them, and re-layouts: 9.13 us -> none  [shards(): return first_sum + second_sum]
    concatenate x1 -> x0, other arithmetic: 7.4 us -> none  [shards(): a_later = jnp.concatenate([a_here[:, inner_count:], moved_tile], axis=1)]
    slice x1 -> x0, local copies, waits for them, and re-layouts: 5.37 us -> none  [shards(): a_later = jnp.concatenate([a_here[:, inner_count:], moved_tile], axis=1)]
  transfers between devices with their start and end apart: 2 -> 5, of which waited for: 1 -> 2; matrix products, arithmetic and copies ran while one was open for 15% -> 0% of each run, Pallas kernels for 0% -> 42%
where the time goes in v1:
time: 39 us; the launch traced here: 38.4 us
  Pallas kernels  18.4 us (47%)
  starting transfers between devices  10.8 us (28%)
  waiting for transfers between devices  8.01 us (21%)
  local copies, waits for them, and re-layouts  1.19 us (3%)
    ppermute x5, starting transfers between devices, passed_along(): return lax.ppermute(value, axis, pairs)  10.8 us
    ppermute x5, waiting for transfers between devices, passed_along(): return lax.ppermute(value, axis, pairs)  8.01 us
    pallas_call x1, Pallas kernels, first(): pl.pallas_call(first_kernel, out_shape=jax.ShapeDtypeStruct((BR, 2 * BC,...  6.66 us
    pallas_call x2, Pallas kernels, add(): pl.pallas_call(functools.partial(add_kernel, first_col), out_shape=jax.Sh...  4.84 us
    pallas_call x2, Pallas kernels, pack(): pl.pallas_call(functools.partial(pack_kernel, rows, cols), out_shape=(slo...  4.22 us
    pallas_call x1, Pallas kernels, later_lists(): pl.pallas_call(later_lists_kernel, out_shape=(lists, lists), in_specs=[SM...  2.64 us
    unnamed x12, local copies, waits for them, and re-layouts  1.19 us
  transfers between devices with their start and end apart: 5, of which 2 were waited for; matrix products, arithmetic and copies ran while one was open for 0% of the time, Pallas kernels for 42%

profile of v1, /device:TPU:0, one launch (start us, length us, event | category | flops | bytes accessed | tf_op | source)
XLA Modules:
  0.0 38.4 jit_solution(2111218193513263274)
XLA Ops:
  0.0 5.0 %collective-permute-start = (s32[8,32]{1,0:T(8,128)}, s32[8,32]{1,0:T(8,128)S(1)}, u32[]{:S(2)}, u32[]{:S(2)}) collective-permute-start(s32[8,32]{1,0:T(8,128)} %a_pattern.3), channel_id=1, source_target_pairs={{0,7},{1,0},{2,1},{3,2},{4,3},{5,4},{6,5},{7,6},{8,15},{9,8},{10,9... | collective-permute-start | bytes 3080 | tf_op jit(solution)/shard_map/ppermute | solution.py:23
  5.1 4.3 %collective-permute-start.1 = (s32[16,16]{1,0:T(8,128)}, s32[16,16]{1,0:T(8,128)S(1)}, u32[]{:S(2)}, u32[]{:S(2)}) collective-permute-start(s32[16,16]{1,0:T(8,128)} %b_pattern.1), channel_id=1, source_target_pairs={{0,120},{8,0},{16,8},{24,16},{32,24},{40,32},{48,40},{56,48},{64,5... | collective-permute-start | bytes 3080 | tf_op jit(solution)/shard_map/ppermute | solution.py:23
  9.4 2.2 %pack.3 = (bf16[16,128,128]{2,1,0:T(8,128)(2,1)S(1)}, bf16[16,128,128]{2,1,0:T(8,128)(2,1)S(1)}) custom-call(s32[16,16]{1,0:T(8,128)} %b_pattern.1, bf16[16,16,128,128]{3,2,1,0:T(8,128)(2,1)} %blocks.3, s32[16,16]{1,0:T(8,128)} %b_pattern.1), custom_call_target="tpu_custom_call" | custom-call | tf_op jit(solution)/shard_map/pack/pallas_call | solution.py:69
  11.6 0.9 %collective-permute-start.3 = (bf16[16,128,128]{2,1,0:T(8,128)(2,1)S(1)}, bf16[16,128,128]{2,1,0:T(8,128)(2,1)S(1)}, u32[]{:S(2)}, u32[]{:S(2)}) collective-permute-start(bf16[16,128,128]{2,1,0:T(8,128)(2,1)S(1)} %get-tuple-element.14.b_1), channel_id=1, source_target_pairs={{0,120},{8,0},{16,8},{24,16},{32,24},{40,32},{48,40},{56,48},{64,5... | collective-permute-start | bytes 1572872 | tf_op jit(solution)/shard_map/ppermute | solution.py:23
  12.5 0.1 collective-permute-start.4
  12.6 0.0 collective-permute-done.a_next
  12.6 0.0 collective-permute-done.1.b_next
  12.6 0.6 %copy-done.5 = s32[8,32]{1,0:T(8,128)} copy-done((s32[8,32]{1,0:T(8,128)}, s32[8,32]{1,0:T(8,128)S(1)}, u32[]{:S(2)}) %copy-start.5) | copy-done | bytes 1048
  13.2 0.6 %copy-done.4 = s32[16,16]{1,0:T(8,128)} copy-done((s32[16,16]{1,0:T(8,128)}, s32[16,16]{1,0:T(8,128)S(1)}, u32[]{:S(2)}) %copy-start.4) | copy-done | bytes 1048
  13.8 2.6 %later_lists.1 = (s32[256]{0:T(256)}, s32[256]{0:T(256)}) custom-call(s32[8,32]{1,0:T(8,128)} %a_pattern.3, s32[8,32]{1,0:T(8,128)} %copy-done.5, s32[16,16]{1,0:T(8,128)} %copy-done.4), custom_call_target="tpu_custom_call" | custom-call | tf_op jit(solution)/shard_map/later_lists/pallas_call | solution.py:142
  16.4 0.0 copy-start.2
  16.4 2.1 %pack.2 = (bf16[16,128,128]{2,1,0:T(8,128)(2,1)S(1)}, bf16[16,128,128]{2,1,0:T(8,128)(2,1)S(1)}) custom-call(s32[8,32]{1,0:T(8,128)} %a_pattern.3, bf16[8,32,128,128]{3,2,1,0:T(8,128)(2,1)} %blocks.2, s32[256]{0:T(256)} %get-tuple-element.12._.pairs), custom_call_target="tpu_custom_call" | custom-call | tf_op jit(solution)/shard_map/pack/pallas_call | solution.py:69
  18.5 0.4 collective-permute-start.2
  18.9 0.0 copy-done.1
  18.9 0.0 copy-done
  18.9 6.7 %first_product.1._ = f32[8,16,128,128]{3,2,1,0:T(8,128)} custom-call(s32[8,32]{1,0:T(8,128)S(1)} %copy-done.1, s32[16,16]{1,0:T(8,128)S(1)} %copy-done, bf16[16,128,128]{2,1,0:T(8,128)(2,1)S(1)} %get-tuple-element.13.a_0, bf16[16,128,128]{2,1,0:T(8,128)(2,1)S(1)} %get-tuple-element.15.a_1.a_slots, bf16[16,128,128]{2,1,0:T(8,128)(2,1)S(1)} %get-tuple-element.16.b_0, ...), custom_call_target="tpu_custom_call" | custom-call | bytes 20971520 | tf_op jit(solution)/shard_map/first_product/pallas_call | solution.py:182
  25.6 0.0 copy-start.3
  25.6 4.6 %collective-permute-done.4.b_slots = bf16[16,128,128]{2,1,0:T(8,128)(2,1)S(1)} collective-permute-done((bf16[16,128,128]{2,1,0:T(8,128)(2,1)S(1)}, bf16[16,128,128]{2,1,0:T(8,128)(2,1)S(1)}, u32[]{:S(2)}, u32[]{:S(2)}) %collective-permute-start.4) | collective-permute-done | bytes 524320 | tf_op jit(solution)/shard_map/ppermute | solution.py:23
  30.2 0.0 copy-done.2
  30.2 2.4 %second_product.2._ = f32[8,16,128,128]{3,2,1,0:T(8,128)} custom-call(s32[256]{0:T(256)S(1)} %copy-done.2, bf16[16,128,128]{2,1,0:T(8,128)(2,1)S(1)} %get-tuple-element.15.a_1.a_slots, bf16[16,128,128]{2,1,0:T(8,128)(2,1)S(1)} %collective-permute-done.4.b_slots, f32[8,16,128,128]{3,2,1,0:T(8,128)} %first_product.1._), custom_call_target="tpu_custom_call", output_to_operand_aliasing={{}: (3, {})} | custom-call | tf_op jit(solution)/shard_map/second_product/pallas_call | solution.py:234
  32.7 0.0 collective-permute-done.3.b_slots
  32.7 3.4 %collective-permute-done.2.a_slots = bf16[16,128,128]{2,1,0:T(8,128)(2,1)S(1)} collective-permute-done((bf16[16,128,128]{2,1,0:T(8,128)(2,1)S(1)}, bf16[16,128,128]{2,1,0:T(8,128)(2,1)S(1)}, u32[]{:S(2)}, u32[]{:S(2)}) %collective-permute-start.2) | collective-permute-done | bytes 524320 | tf_op jit(solution)/shard_map/ppermute | solution.py:23
  36.0 0.0 copy-done.3
  36.0 2.4 %second_product.3 = f32[8,16,128,128]{3,2,1,0:T(8,128)} custom-call(s32[256]{0:T(256)S(1)} %copy-done.3, bf16[16,128,128]{2,1,0:T(8,128)(2,1)S(1)} %collective-permute-done.2.a_slots, bf16[16,128,128]{2,1,0:T(8,128)(2,1)S(1)} %collective-permute-done.3.b_slots, f32[8,16,128,128]{3,2,1,0:T(8,128)} %second_product.2._), custom_call_target="tpu_custom_call", output_to_operand_aliasing={{}: (3, {})} | custom-call | tf_op jit(solution)/shard_map/second_product/pallas_call | solution.py:234
  (4 shorter events, 0.0 us)
Async XLA Ops:
  0.0 18.9 %copy-start.1 = (s32[8,32]{1,0:T(8,128)S(1)}, s32[8,32]{1,0:T(8,128)}, u32[]{:S(2)}) copy-start(s32[8,32]{1,0:T(8,128)} %a_pattern.3) | copy-start | bytes 3076
  0.0 18.9 %copy-start = (s32[16,16]{1,0:T(8,128)S(1)}, s32[16,16]{1,0:T(8,128)}, u32[]{:S(2)}) copy-start(s32[16,16]{1,0:T(8,128)} %b_pattern.1) | copy-start | bytes 3076
  0.0 12.6 %collective-permute-start = (s32[8,32]{1,0:T(8,128)}, s32[8,32]{1,0:T(8,128)S(1)}, u32[]{:S(2)}, u32[]{:S(2)}) collective-permute-start(s32[8,32]{1,0:T(8,128)} %a_pattern.3), channel_id=1, source_target_pairs={{0,7},{1,0},{2,1},{3,2},{4,3},{5,4},{6,5},{7,6},{8,15},{9,8},{10,9... | collective-permute-start | bytes 3080 | tf_op jit(solution)/shard_map/ppermute | solution.py:23
  5.1 7.5 %collective-permute-start.1 = (s32[16,16]{1,0:T(8,128)}, s32[16,16]{1,0:T(8,128)S(1)}, u32[]{:S(2)}, u32[]{:S(2)}) collective-permute-start(s32[16,16]{1,0:T(8,128)} %b_pattern.1), channel_id=1, source_target_pairs={{0,120},{8,0},{16,8},{24,16},{32,24},{40,32},{48,40},{56,48},{64,5... | collective-permute-start | bytes 3080 | tf_op jit(solution)/shard_map/ppermute | solution.py:23
  11.6 21.1 %collective-permute-start.3 = (bf16[16,128,128]{2,1,0:T(8,128)(2,1)S(1)}, bf16[16,128,128]{2,1,0:T(8,128)(2,1)S(1)}, u32[]{:S(2)}, u32[]{:S(2)}) collective-permute-start(bf16[16,128,128]{2,1,0:T(8,128)(2,1)S(1)} %get-tuple-element.14.b_1), channel_id=1, source_target_pairs={{0,120},{8,0},{16,8},{24,16},{32,24},{40,32},{48,40},{56,48},{64,5... | collective-permute-start | bytes 1572872 | tf_op jit(solution)/shard_map/ppermute | solution.py:23
  12.5 17.7 %collective-permute-start.4 = (bf16[16,128,128]{2,1,0:T(8,128)(2,1)S(1)}, bf16[16,128,128]{2,1,0:T(8,128)(2,1)S(1)}, u32[]{:S(2)}, u32[]{:S(2)}) collective-permute-start(bf16[16,128,128]{2,1,0:T(8,128)(2,1)S(1)} %get-tuple-element.16.b_0), channel_id=1, source_target_pairs={{0,120},{8,0},{16,8},{24,16},{32,24},{40,32},{48,40},{56,48},{64,5... | collective-permute-start | bytes 1572872 | tf_op jit(solution)/shard_map/ppermute | solution.py:23
  12.6 0.6 %copy-start.5 = (s32[8,32]{1,0:T(8,128)}, s32[8,32]{1,0:T(8,128)S(1)}, u32[]{:S(2)}) copy-start(s32[8,32]{1,0:T(8,128)S(1)} %collective-permute-done.a_next) | copy-start | bytes 3076
  13.2 0.6 %copy-start.4 = (s32[16,16]{1,0:T(8,128)}, s32[16,16]{1,0:T(8,128)S(1)}, u32[]{:S(2)}) copy-start(s32[16,16]{1,0:T(8,128)S(1)} %collective-permute-done.1.b_next) | copy-start | bytes 3076
  16.4 13.8 %copy-start.2 = (s32[256]{0:T(256)S(1)}, s32[256]{0:T(256)}, u32[]{:S(2)}) copy-start(s32[256]{0:T(256)} %get-tuple-element.12._.pairs) | copy-start | bytes 3076
  18.5 17.5 %collective-permute-start.2 = (bf16[16,128,128]{2,1,0:T(8,128)(2,1)S(1)}, bf16[16,128,128]{2,1,0:T(8,128)(2,1)S(1)}, u32[]{:S(2)}, u32[]{:S(2)}) collective-permute-start(bf16[16,128,128]{2,1,0:T(8,128)(2,1)S(1)} %get-tuple-element.13.a_0), channel_id=1, source_target_pairs={{0,7},{1,0},{2,1},{3,2},{4,3},{5,4},{6,5},{7,6},{8,15},{9,8},{10,9... | collective-permute-start | bytes 1572872 | tf_op jit(solution)/shard_map/ppermute | solution.py:23
  25.6 10.5 %copy-start.3 = (s32[256]{0:T(256)S(1)}, s32[256]{0:T(256)}, u32[]{:S(2)}) copy-start(s32[256]{0:T(256)} %get-tuple-element.11.pairs) | copy-start | bytes 3076

commit v2 on v0

v2 whole, which is shorter than its diff:
```python
import functools

import jax
import jax.numpy as jnp
from jax import lax
from jax.experimental import pallas as pl
from jax.experimental.pallas import tpu as pltpu
from jax.sharding import PartitionSpec as P

BR, KS, BC = 8, 16, 8
CAP = 16
BLOCK = 128
B_SENT = 8
A_PART = 8
MARKS = 16
UNROLL = 4
PAIRS, TOUCHED, PLACES, LIST = 8, 144, 208, 256
ANY = pl.BlockSpec(memory_space=pl.ANY)
SMEM = pl.BlockSpec(memory_space=pltpu.SMEM)
VMEM = pl.BlockSpec(memory_space=pltpu.VMEM)


def passed_along(value, axis, steps, senders=None):
    count = lax.axis_size(axis)
    pairs = [(source, (source + steps) % count) for source in range(count)]
    return lax.ppermute(value, axis, pairs if senders is None else pairs[senders::2])


def rows_of(slot, count=1):
    return pl.ds(pl.multiple_of(slot * BLOCK, BLOCK), count * BLOCK)


def scan(pattern, first_col, rows, cols, places, starts=None):
    count = jnp.int32(0)
    for row in range(rows):
        if starts is not None:
            starts[row] = count
        for col in range(cols):
            places[count] = row * cols + col
            count = count + pattern[row, first_col + col]
    if starts is not None:
        starts[rows] = count
    return count


def fetch(first, last, first_col, cols, source, places, target, first_slot, sem):
    def start(index, carry):
        place = places[index]
        block = source.at[place // cols, first_col + place % cols]
        pltpu.make_async_copy(block, target.at[rows_of(first_slot + index - first)], sem).start()
        return carry

    lax.fori_loop(first, last, start, 0)


def write_marks(pattern, marks, target, sem):
    rows, cols = pattern.shape
    marks[...] = jnp.zeros(marks.shape, marks.dtype)
    marks[:rows, :cols] = pattern[...].astype(jnp.float32).astype(marks.dtype)
    copy = pltpu.make_async_copy(marks, target.at[pl.ds(target.shape[0] - MARKS, MARKS)], sem)
    copy.start()
    return copy


def drain(count, source, target, sem):
    def wait(_, carry):
        pltpu.make_async_copy(source, target, sem).wait()
        return carry

    lax.fori_loop(0, count, wait, 0)


def pack_b_kernel(pattern, pattern_held, blocks, sent, extra, info, places_0, places_1, marks, sem, marks_sem):
    copy = write_marks(pattern_held, marks, sent, marks_sem)
    count_0 = scan(pattern, 0, KS, BC, places_0)
    fetch(0, count_0, 0, BC, blocks, places_0, sent, 0, sem)
    count_1 = scan(pattern, BC, KS, BC, places_1)
    fetch(0, jnp.minimum(count_1, B_SENT), BC, BC, blocks, places_1, sent, 2 * B_SENT, sem)
    rest_0 = jnp.maximum(count_0 - B_SENT, 0)
    rest = rest_0 + jnp.maximum(count_1 - B_SENT, 0)
    last = jnp.minimum(count_1, 2 * B_SENT - rest_0)
    fetch(B_SENT, last, BC, BC, blocks, places_1, sent, B_SENT + rest_0, sem)
    fetch(jnp.maximum(last, B_SENT), count_1, BC, BC, blocks, places_1, extra, 0, sem)
    info[0] = (rest > B_SENT).astype(jnp.int32)
    drain(count_0 + count_1, blocks.at[0, 0], sent.at[rows_of(0)], sem)
    copy.wait()


def slots(count, marks=0):
    return pltpu.VMEM((count * BLOCK + marks, BLOCK), jnp.bfloat16)


INFO = jax.ShapeDtypeStruct((8,), jnp.int32)
PACK_PARAMS = pltpu.CompilerParams(vmem_limit_bytes=56 * 2**20)


def pack_b(blocks, pattern):
    return pl.pallas_call(
        pack_b_kernel,
        out_shape=(slots(3 * B_SENT, MARKS), slots(B_SENT), INFO),
        in_specs=[SMEM, VMEM, ANY],
        out_specs=(ANY, ANY, SMEM),
        scratch_shapes=[
            pltpu.SMEM((CAP + 1,), jnp.int32),
            pltpu.SMEM((CAP + 1,), jnp.int32),
            pltpu.VMEM((MARKS, BLOCK), jnp.bfloat16),
            pltpu.SemaphoreType.DMA,
            pltpu.SemaphoreType.DMA,
        ],
        compiler_params=PACK_PARAMS,
        name="pack_b",
    )(pattern, pattern, blocks)


def pack_a_kernel(pattern, pattern_held, blocks, part_0, part_1, places, marks, sems):
    copy = write_marks(pattern_held, marks, part_0, sems.at[1])
    count = scan(pattern, 0, BR, KS, places)
    fetch(0, jnp.minimum(count, A_PART), 0, KS, blocks, places, part_0, 0, sems.at[0])
    fetch(A_PART, count, 0, KS, blocks, places, part_1, 0, sems.at[0])
    drain(count, blocks.at[0, 0], part_1.at[rows_of(0)], sems.at[0])
    copy.wait()


def pack_a(blocks, pattern):
    return pl.pallas_call(
        pack_a_kernel,
        out_shape=(slots(A_PART, MARKS), slots(CAP - A_PART)),
        in_specs=[SMEM, VMEM, ANY],
        out_specs=(ANY, ANY),
        scratch_shapes=[
            pltpu.SMEM((CAP + 1,), jnp.int32),
            pltpu.VMEM((MARKS, BLOCK), jnp.bfloat16),
            pltpu.SemaphoreType.DMA((2,)),
        ],
        compiler_params=PACK_PARAMS,
        name="pack_a",
    )(pattern, pattern, blocks)


def list_pairs(a_count, a_places, b_places, b_starts, b_slot_of, out, seen):
    for place in range(BR * BC):
        seen[place] = 0

    def over_a(a_slot, counts):
        place = a_places[a_slot]
        row, inner = place // KS, place % KS

        def over_b(b_index, counts):
            pairs, touched = counts
            target = row * BC + b_places[b_index] % BC
            out[PAIRS + pairs] = a_slot + b_slot_of(b_index) * 256 + target * 65536
            out[TOUCHED + touched] = target
            touched = touched + 1 - seen[target]
            seen[target] = 1
            return pairs + 1, touched

        return lax.fori_loop(b_starts[inner], b_starts[inner + 1], over_b, counts)

    pairs, touched = lax.fori_loop(0, a_count, over_a, (jnp.int32(0), jnp.int32(0)))
    for extra in range(UNROLL - 1):
        out[PAIRS + pairs + extra] = BR * BC * 65536
    out[0] = (pairs + UNROLL - 1) // UNROLL
    out[1] = touched
    out[3] = a_count


LIST_SCRATCH = [
    pltpu.SMEM((CAP + 1,), jnp.int32),
    pltpu.SMEM((CAP + 1,), jnp.int32),
    pltpu.SMEM((KS + 1,), jnp.int32),
    pltpu.SMEM((BR * BC,), jnp.int32),
]


def rest_sent(flags, extra):
    def sent(senders, flag):
        return lax.cond(
            flag != 0,
            lambda value: passed_along(value, "row", -1, senders),
            jnp.zeros_like,
            extra,
        )

    def some(extra):
        return sent(1, flags[1]) + sent(0, flags[2])

    return lax.cond(flags[0] != 0, some, lambda extra: extra, extra)


def multiply(pairs, a_slots, b_slots, total, first_col):
    def step(index, carry):
        products = []
        for part in range(UNROLL):
            pair = pairs[PAIRS + index * UNROLL + part]
            a_slot, b_slot, target = pair % 256, (pair // 256) % 256, pair // 65536
            product = jnp.dot(
                a_slots[rows_of(a_slot), :], b_slots[rows_of(b_slot), :], preferred_element_type=jnp.float32
            )
            products.append((target // BC, first_col + target % BC, product))
        for row, col, product in products:
            total[row, col] += product
        return carry

    lax.fori_loop(0, pairs[0], step, 0)


def first_kernel(
    a_pattern, b_pattern, a_blocks, b_blocks, result,
    zeros, total, a_held, b_held, own_0, own_1, sems, a_places, b_places, b_starts, seen,
):
    zeros[...] = jnp.zeros(zeros.shape, zeros.dtype)
    clears = [pltpu.make_async_copy(zeros, result.at[row], sems.at[2]) for row in range(BR)]
    for clear in clears:
        clear.start()
    lists = (own_0, own_1)
    counts = []
    for tile, out in enumerate(lists):
        a_count = scan(a_pattern, tile * KS, BR, KS, a_places)
        fetch(0, a_count, tile * KS, KS, a_blocks, a_places, a_held.at[tile], 0, sems.at[tile])
        b_count = scan(b_pattern, tile * BC, KS, BC, b_places, starts=b_starts)
        fetch(0, b_count, tile * BC, BC, b_blocks, b_places, b_held.at[tile], 0, sems.at[tile])
        counts.append(a_count + b_count)
        list_pairs(a_count, a_places, b_places, b_starts, lambda index: index, out, seen)

        def clear(index, carry):
            target = out[TOUCHED + index]
            total[target // BC, tile * BC + target % BC] = jnp.zeros((BLOCK, BLOCK), total.dtype)
            return carry

        lax.fori_loop(0, out[1], clear, 0)
    for tile, out in enumerate(lists):
        drain(counts[tile], a_blocks.at[0, 0], a_held.at[0, rows_of(0)], sems.at[tile])
        multiply(out, a_held.at[tile], b_held.at[tile], total, tile * BC)
    for clear in clears:
        clear.wait()
    for tile, out in enumerate(lists):

        def store(index, carry):
            target = out[TOUCHED + index]
            row, col = target // BC, tile * BC + target % BC
            pltpu.make_async_copy(total.at[row, col], result.at[row, col], sems.at[3]).start()
            return carry

        lax.fori_loop(0, out[1], store, 0)
    drain(own_0[1] + own_1[1], total.at[0, 0], result.at[0, 0], sems.at[3])


def first(a_pattern, b_pattern, a_blocks, b_blocks):
    return pl.pallas_call(
        first_kernel,
        out_shape=jax.ShapeDtypeStruct((BR, 2 * BC, BLOCK, BLOCK), jnp.float32),
        in_specs=[SMEM, SMEM, ANY, ANY],
        out_specs=ANY,
        scratch_shapes=[
            pltpu.VMEM((2 * BC, BLOCK, BLOCK), jnp.float32),
            pltpu.VMEM((BR + 1, 2 * BC, BLOCK, BLOCK), jnp.float32),
            pltpu.VMEM((2, CAP * BLOCK, BLOCK), jnp.bfloat16),
            pltpu.VMEM((2, CAP * BLOCK, BLOCK), jnp.bfloat16),
            pltpu.SMEM((LIST,), jnp.int32),
            pltpu.SMEM((LIST,), jnp.int32),
            pltpu.SemaphoreType.DMA((4,)),
            *LIST_SCRATCH,
        ],
        compiler_params=pltpu.CompilerParams(vmem_limit_bytes=52 * 2**20),
        cost_estimate=pl.CostEstimate(flops=0, bytes_accessed=20 * 2**20, transcendentals=0),
        name="first_product",
    )(a_pattern, b_pattern, a_blocks, b_blocks)


def touched_blocks(pairs, first_col, result, total):
    def block(index):
        target = pairs[TOUCHED + index]
        row, col = target // BC, target % BC
        return result.at[row, first_col + col], total.at[row, col]

    def load(sem):
        def start(index, carry):
            there, here = block(index)
            pltpu.make_async_copy(there, here, sem).start()
            return carry

        lax.fori_loop(0, pairs[1], start, 0)

    def store(sem):
        def start(index, carry):
            there, here = block(index)
            pltpu.make_async_copy(here, there, sem).start()
            return carry

        lax.fori_loop(0, pairs[1], start, 0)

    return load, store


def read_marks(sent, marks, turned, sems):
    load = pltpu.make_async_copy(sent.at[pl.ds(sent.shape[0] - MARKS, MARKS)], marks, sems.at[0])
    load.start()

    def finish(pattern):
        load.wait()
        turned[...] = marks[...].astype(jnp.float32).astype(jnp.int32)
        copy = pltpu.make_async_copy(turned, pattern, sems.at[1])
        copy.start()
        copy.wait()

    return finish


READ_SCRATCH = [
    pltpu.VMEM((MARKS, BLOCK), jnp.bfloat16),
    pltpu.VMEM((MARKS, BLOCK), jnp.int32),
    pltpu.SMEM((MARKS, BLOCK), jnp.int32),
    pltpu.SemaphoreType.DMA((2,)),
]
B_PLACES, B_REST = 24, 48


def middle_kernel(
    a_pattern, b_info, b_sent, a_blocks, _, result, b_list, flags,
    total, a_held, b_held, pairs, marks, turned, b_next, mark_sems, sems, a_places, b_places, b_starts, seen,
):
    finish = read_marks(b_sent, marks, turned, mark_sems)
    load_b = pltpu.make_async_copy(b_sent.at[rows_of(0, 2 * B_SENT)], b_held, sems.at[0])
    load_b.start()
    a_count = scan(a_pattern, KS, BR, KS, a_places)
    fetch(0, a_count, KS, KS, a_blocks, a_places, a_held, 0, sems.at[1])
    finish(b_next)
    count_0 = scan(b_next, 0, KS, BC, b_places, starts=b_starts)
    list_pairs(a_count, a_places, b_places, b_starts, lambda index: index, pairs, seen)
    load, store = touched_blocks(pairs, 0, result, total)
    load(sems.at[2])

    count_1 = scan(b_next, BC, KS, BC, b_places, starts=b_starts)
    for row in range(KS + 1):
        b_list[row] = b_starts[row]
    for index in range(CAP):
        b_list[B_PLACES + index] = b_places[index]
    rest_0 = jnp.maximum(count_0 - B_SENT, 0)
    rest = rest_0 + jnp.maximum(count_1 - B_SENT, 0)
    b_list[B_REST] = rest_0
    goes, comes = b_info[0], (rest > B_SENT).astype(jnp.int32)
    odd_row = lax.axis_index("row") % 2 == 1
    flags[0] = goes | comes
    flags[1] = jnp.where(odd_row, goes, comes)
    flags[2] = jnp.where(odd_row, comes, goes)
    b_list[B_REST + 1] = comes

    load_b.wait()
    drain(a_count, a_blocks.at[0, 0], a_held.at[rows_of(0)], sems.at[1])
    drain(pairs[1], result.at[0, 0], total.at[0, 0], sems.at[2])
    multiply(pairs, a_held, b_held, total, 0)
    store(sems.at[3])
    drain(pairs[1], total.at[0, 0], result.at[0, 0], sems.at[3])


def middle(a_pattern, b_info, b_sent, a_blocks, result):
    return pl.pallas_call(
        middle_kernel,
        out_shape=(
            jax.ShapeDtypeStruct(result.shape, result.dtype),
            jax.ShapeDtypeStruct((64,), jnp.int32),
            INFO,
        ),
        in_specs=[SMEM, SMEM, ANY, ANY, ANY],
        out_specs=(ANY, SMEM, SMEM),
        scratch_shapes=[
            pltpu.VMEM((BR + 1, BC, BLOCK, BLOCK), jnp.float32),
            pltpu.VMEM((CAP * BLOCK, BLOCK), jnp.bfloat16),
            pltpu.VMEM((2 * B_SENT * BLOCK, BLOCK), jnp.bfloat16),
            pltpu.SMEM((LIST,), jnp.int32),
            *READ_SCRATCH,
            pltpu.SemaphoreType.DMA((4,)),
            *LIST_SCRATCH,
        ],
        input_output_aliases={4: 0},
        compiler_params=pltpu.CompilerParams(vmem_limit_bytes=40 * 2**20),
        name="second_product_first_tile",
    )(a_pattern, b_info, b_sent, a_blocks, result)


def last_list_kernel(b_list, a_sent, pairs, marks, turned, a_next, mark_sems, a_places, seen):
    finish = read_marks(a_sent, marks, turned, mark_sems)
    finish(a_next)
    a_count = scan(a_next, 0, BR, KS, a_places)
    rest_0 = b_list[B_REST]

    def b_slot_of(index):
        past = rest_0 + index - B_SENT
        later = jnp.where(past < B_SENT, past + B_SENT, past + 2 * B_SENT)
        return jnp.where(index < B_SENT, index + 2 * B_SENT, later)

    list_pairs(a_count, a_places, b_list.at[pl.ds(B_PLACES, CAP)], b_list, b_slot_of, pairs, seen)
    pairs[2] = b_list[B_REST + 1]


def last_list(b_list, a_sent):
    return pl.pallas_call(
        last_list_kernel,
        out_shape=jax.ShapeDtypeStruct((LIST,), jnp.int32),
        in_specs=[SMEM, ANY],
        out_specs=SMEM,
        scratch_shapes=[
            *READ_SCRATCH,
            pltpu.SMEM((CAP + 1,), jnp.int32),
            pltpu.SMEM((BR * BC,), jnp.int32),
        ],
        compiler_params=pltpu.CompilerParams(vmem_limit_bytes=16 * 2**20),
        name="last_list",
    )(b_list, a_sent)


def last_kernel(pairs, a_0, a_1, b_0, b_1, _, result, total, a_held, b_held, sems):
    loads = [
        pltpu.make_async_copy(a_0.at[rows_of(0, A_PART)], a_held.at[rows_of(0, A_PART)], sems.at[2]),
        pltpu.make_async_copy(a_1, a_held.at[rows_of(A_PART, CAP - A_PART)], sems.at[3]),
        pltpu.make_async_copy(
            b_0.at[rows_of(B_SENT, 2 * B_SENT)], b_held.at[rows_of(B_SENT, 2 * B_SENT)], sems.at[4]
        ),
    ]
    for each in loads:
        each.start()
    load, store = touched_blocks(pairs, BC, result, total)
    load(sems.at[0])

    @pl.when(pairs[2] != 0)
    def _():
        extra = pltpu.make_async_copy(b_1, b_held.at[rows_of(3 * B_SENT, B_SENT)], sems.at[5])
        extra.start()
        extra.wait()

    for each in loads:
        each.wait()
    drain(pairs[1], result.at[0, 0], total.at[0, 0], sems.at[0])
    multiply(pairs, a_held, b_held, total, 0)
    store(sems.at[1])
    drain(pairs[1], total.at[0, 0], result.at[0, 0], sems.at[1])


def last(pairs, a_0, a_1, b_0, b_1, result):
    return pl.pallas_call(
        last_kernel,
        out_shape=jax.ShapeDtypeStruct(result.shape, result.dtype),
        in_specs=[SMEM] + [ANY] * 5,
        out_specs=ANY,
        scratch_shapes=[
            pltpu.VMEM((BR + 1, BC, BLOCK, BLOCK), jnp.float32),
            pltpu.VMEM((CAP * BLOCK, BLOCK), jnp.bfloat16),
            pltpu.VMEM((4 * B_SENT * BLOCK, BLOCK), jnp.bfloat16),
            pltpu.SemaphoreType.DMA((6,)),
        ],
        input_output_aliases={5: 0},
        compiler_params=pltpu.CompilerParams(vmem_limit_bytes=16 * 2**20),
        name="second_product_second_tile",
    )(pairs, a_0, a_1, b_0, b_1, result)


def shards(a_blocks, a_pattern, b_blocks, b_pattern):
    b_sent, b_extra, b_info = pack_b(b_blocks, b_pattern)
    b_sent = passed_along(b_sent, "row", -1)
    a_sent_0, a_sent_1 = pack_a(a_blocks, a_pattern)
    a_sent_0 = passed_along(a_sent_0, "col", -1)
    result = first(a_pattern, b_pattern, a_blocks, b_blocks)
    a_sent_1, b_sent, result = lax.optimization_barrier((a_sent_1, b_sent, result))
    a_sent_1 = passed_along(a_sent_1, "col", -1)
    result, b_list, flags = middle(a_pattern, b_info, b_sent, a_blocks, result)
    b_extra = rest_sent(flags, b_extra)
    pairs = last_list(b_list, a_sent_0)
    return last(pairs, a_sent_0, a_sent_1, b_sent, b_extra, result)


def solution(mesh):
    return jax.shard_map(
        shards,
        mesh=mesh,
        in_specs=(
            P("row", "col", None, None),
            P("row", "col"),
            P("row", "col", None, None),
            P("row", "col"),
        ),
        out_specs=P("row", "col", None, None),
        check_vma=False,
    )
```

time: 242 us -> 34.7 us (0.14)
  the two profiles are of different devices: /device:TPU:0 before, /device:TPU:13 now
where the time goes in v2:
time: 34.7 us; the launch traced here: 34.5 us
  Pallas kernels  20.1 us (58%)
  starting transfers between devices  9.56 us (28%)
  waiting for transfers between devices  4.72 us (14%)
    ppermute x3, starting transfers between devices, passed_along(): lax.ppermute(value, axis, pairs if senders is None else pairs[senders::2])  9.56 us
    pallas_call x1, Pallas kernels, middle(): pl.pallas_call(middle_kernel, out_shape=(jax.ShapeDtypeStruct(result.shap...  5.89 us
    pallas_call x1, Pallas kernels, first(): pl.pallas_call(first_kernel, out_shape=jax.ShapeDtypeStruct((BR, 2 * BC,...  5.07 us
    ppermute x3, waiting for transfers between devices, passed_along(): lax.ppermute(value, axis, pairs if senders is None else pairs[senders::2])  4.72 us
    pallas_call x1, Pallas kernels, pack_b(): pl.pallas_call(pack_b_kernel, out_shape=(slots(3 * B_SENT, MARKS), slots(...  2.78 us
    pallas_call x1, Pallas kernels, last(): pl.pallas_call(last_kernel, out_shape=jax.ShapeDtypeStruct(result.shape,...  2.37 us
    pallas_call x1, Pallas kernels, last_list(): pl.pallas_call(last_list_kernel, out_shape=jax.ShapeDtypeStruct((LIST,),...  2.17 us
    pallas_call x1, Pallas kernels, pack_a(): pl.pallas_call(pack_a_kernel, out_shape=(slots(A_PART, MARKS), slots(CAP...  1.82 us
  transfers between devices with their start and end apart: 3, of which 1 were waited for; matrix products, arithmetic and copies ran while one was open for 0% of the time, Pallas kernels for 43%

profile of v2, /device:TPU:13, one launch (start us, length us, event | category | flops | bytes accessed | tf_op | source)
XLA Modules:
  0.0 34.5 jit_solution(6850098109929471209)
XLA Ops:
  0.0 0.0 copy-start
  0.0 0.0 copy-start.1
  0.0 2.8 %pack_b.1 = (bf16[3088,128]{1,0:T(8,128)(2,1)S(1)}, bf16[1024,128]{1,0:T(8,128)(2,1)S(1)}, s32[8]{0:T(128)}) custom-call(s32[16,16]{1,0:T(8,128)} %b_pattern.1, s32[16,16]{1,0:T(8,128)} %b_pattern.1, bf16[16,16,128,128]{3,2,1,0:T(8,128)(2,1)} %b_blocks.1), custom_call_target="tpu_custom_call" | custom-call | tf_op jit(solution)/shard_map/pack_b/pallas_call | solution.py:98
  2.8 0.7 %collective-permute-start.2 = (bf16[3088,128]{1,0:T(8,128)(2,1)S(1)}, bf16[3088,128]{1,0:T(8,128)(2,1)S(1)}, u32[]{:S(2)}, u32[]{:S(2)}) collective-permute-start(bf16[3088,128]{1,0:T(8,128)(2,1)S(1)} %get-tuple-element.36), channel_id=1, source_target_pairs={{0,120},{8,0},{16,8},{24,16},{32,24},{40,32},{48,40},{56,48},{64,5... | collective-permute-start | bytes 2371592 | tf_op jit(solution)/shard_map/ppermute | solution.py:26
  3.5 1.8 %pack_a.1 = (bf16[1040,128]{1,0:T(8,128)(2,1)S(1)}, bf16[1024,128]{1,0:T(8,128)(2,1)S(1)}) custom-call(s32[8,32]{1,0:T(8,128)} %a_pattern.3, s32[8,32]{1,0:T(8,128)} %a_pattern.3, bf16[8,32,128,128]{3,2,1,0:T(8,128)(2,1)} %a_blocks.3), custom_call_target="tpu_custom_call" | custom-call | tf_op jit(solution)/shard_map/pack_a/pallas_call | solution.py:125
  5.4 0.0 slice-start
  5.4 0.0 slice-start.1
  5.4 0.0 copy-start.2
  5.4 4.4 %collective-permute-start.3 = (bf16[1040,128]{1,0:T(8,128)(2,1)S(1)}, bf16[1040,128]{1,0:T(8,128)(2,1)S(1)}, u32[]{:S(2)}, u32[]{:S(2)}) collective-permute-start(bf16[1040,128]{1,0:T(8,128)(2,1)S(1)} %get-tuple-element.40), channel_id=1, source_target_pairs={{0,7},{1,0},{2,1},{3,2},{4,3},{5,4},{6,5},{7,6},{8,15},{9,8},{10,9... | collective-permute-start | bytes 798728 | tf_op jit(solution)/shard_map/ppermute | solution.py:26
  9.8 0.0 copy-done
  9.8 0.0 copy-done.1
  9.8 5.1 %first_product.1._ = f32[8,16,128,128]{3,2,1,0:T(8,128)} custom-call(s32[8,32]{1,0:T(8,128)S(1)} %copy-done.1, s32[16,16]{1,0:T(8,128)S(1)} %copy-done, bf16[8,32,128,128]{3,2,1,0:T(8,128)(2,1)} %a_blocks.3, bf16[16,16,128,128]{3,2,1,0:T(8,128)(2,1)} %b_blocks.1), custom_call_target="tpu_custom_call" | custom-call | bytes 20971520 | tf_op jit(solution)/shard_map/first_product/pallas_call | solution.py:249
  14.9 4.7 %collective-permute-done.2.b_sent.b_0 = bf16[3088,128]{1,0:T(8,128)(2,1)S(1)} collective-permute-done((bf16[3088,128]{1,0:T(8,128)(2,1)S(1)}, bf16[3088,128]{1,0:T(8,128)(2,1)S(1)}, u32[]{:S(2)}, u32[]{:S(2)}) %collective-permute-start.2) | collective-permute-done | bytes 790560 | tf_op jit(solution)/shard_map/ppermute | solution.py:26
  19.6 4.4 %collective-permute-start.4 = (bf16[1024,128]{1,0:T(8,128)(2,1)S(1)}, bf16[1024,128]{1,0:T(8,128)(2,1)S(1)}, u32[]{:S(2)}, u32[]{:S(2)}) collective-permute-start(bf16[1024,128]{1,0:T(8,128)(2,1)S(1)} %get-tuple-element.41), channel_id=1, source_target_pairs={{0,7},{1,0},{2,1},{3,2},{4,3},{5,4},{6,5},{7,6},{8,15},{9,8},{10,9... | collective-permute-start | bytes 786440 | tf_op jit(solution)/shard_map/ppermute | solution.py:26
  24.0 0.0 slice-done
  24.0 0.0 slice-done.1
  24.0 0.0 copy-done.2
  24.0 5.9 %second_product_first_tile.1 = (f32[8,16,128,128]{3,2,1,0:T(8,128)}, s32[64]{0:T(128)S(1)}, s32[8]{0:T(128)S(1)}) custom-call(s32[8,32]{1,0:T(8,128)S(1)} %copy-done.1, s32[8]{0:T(128)S(1)} %copy-done.2, bf16[3088,128]{1,0:T(8,128)(2,1)S(1)} %collective-permute-done.2.b_sent.b_0, ...), custom_call_target="tpu_custom_call", output_to_operand_aliasing={{0}: (4, {})} | custom-call | tf_op jit(solution)/shard_map/second_product_first_tile/pallas_call | solution.py:357
  30.0 0.0 collective-permute-done.3.a_sent.a_0
  30.0 2.2 %last_list.1.pairs = s32[256]{0:T(256)S(1)} custom-call(s32[64]{0:T(128)S(1)} %get-tuple-element.39.b_list, bf16[1040,128]{1,0:T(8,128)(2,1)S(1)} %collective-permute-done.3.a_sent.a_0), custom_call_target="tpu_custom_call" | custom-call | tf_op jit(solution)/shard_map/last_list/pallas_call | solution.py:397
  32.2 0.0 collective-permute-done.4.a_1
  32.2 2.4 %second_product_second_tile.1 = f32[8,16,128,128]{3,2,1,0:T(8,128)} custom-call(s32[256]{0:T(256)S(1)} %last_list.1.pairs, bf16[1040,128]{1,0:T(8,128)(2,1)S(1)} %collective-permute-done.3.a_sent.a_0, bf16[1024,128]{1,0:T(8,128)(2,1)S(1)} %collective-permute-done.4.a_1, ...), custom_call_target="tpu_custom_call", output_to_operand_aliasing={{}: (5, {})} | custom-call | tf_op jit(solution)/shard_map/second_product_second_tile/pallas_call | solution.py:440
  (2 shorter events, 0.0 us)
Async XLA Ops:
  0.0 9.8 %copy-start = (s32[16,16]{1,0:T(8,128)S(1)}, s32[16,16]{1,0:T(8,128)}, u32[]{:S(2)}) copy-start(s32[16,16]{1,0:T(8,128)} %b_pattern.1) | copy-start | bytes 3076
  0.0 9.8 %copy-start.1 = (s32[8,32]{1,0:T(8,128)S(1)}, s32[8,32]{1,0:T(8,128)}, u32[]{:S(2)}) copy-start(s32[8,32]{1,0:T(8,128)} %a_pattern.3) | copy-start | bytes 3076
  2.8 16.8 %collective-permute-start.2 = (bf16[3088,128]{1,0:T(8,128)(2,1)S(1)}, bf16[3088,128]{1,0:T(8,128)(2,1)S(1)}, u32[]{:S(2)}, u32[]{:S(2)}) collective-permute-start(bf16[3088,128]{1,0:T(8,128)(2,1)S(1)} %get-tuple-element.36), channel_id=1, source_target_pairs={{0,120},{8,0},{16,8},{24,16},{32,24},{40,32},{48,40},{56,48},{64,5... | collective-permute-start | bytes 2371592 | tf_op jit(solution)/shard_map/ppermute | solution.py:26
  5.4 18.7 %slice-start = ((s8[8388608]{0:T(1024)(128)(4,1)}), s8[4194304]{0:T(1024)(128)(4,1)S(1)}, s32[]{:S(2)}) async-start(s8[8388608]{0:T(1024)(128)(4,1)} %bitcast.4), calls=%async_computation | async-start | bytes 8388608
  5.4 18.6 %slice-start.1 = ((s8[8388608]{0:T(1024)(128)(4,1)}), s8[4194304]{0:T(1024)(128)(4,1)S(1)}, s32[]{:S(2)}) async-start(s8[8388608]{0:T(1024)(128)(4,1)} %bitcast.4), calls=%async_computation.1 | async-start | bytes 8388608
  5.4 18.6 %copy-start.2 = (s32[8]{0:T(128)S(1)}, s32[8]{0:T(128)}, u32[]{:S(2)}) copy-start(s32[8]{0:T(128)} %get-tuple-element.34.b_info) | copy-start | bytes 100
  5.4 24.6 %collective-permute-start.3 = (bf16[1040,128]{1,0:T(8,128)(2,1)S(1)}, bf16[1040,128]{1,0:T(8,128)(2,1)S(1)}, u32[]{:S(2)}, u32[]{:S(2)}) collective-permute-start(bf16[1040,128]{1,0:T(8,128)(2,1)S(1)} %get-tuple-element.40), channel_id=1, source_target_pairs={{0,7},{1,0},{2,1},{3,2},{4,3},{5,4},{6,5},{7,6},{8,15},{9,8},{10,9... | collective-permute-start | bytes 798728 | tf_op jit(solution)/shard_map/ppermute | solution.py:26
  19.6 12.6 %collective-permute-start.4 = (bf16[1024,128]{1,0:T(8,128)(2,1)S(1)}, bf16[1024,128]{1,0:T(8,128)(2,1)S(1)}, u32[]{:S(2)}, u32[]{:S(2)}) collective-permute-start(bf16[1024,128]{1,0:T(8,128)(2,1)S(1)} %get-tuple-element.41), channel_id=1, source_target_pairs={{0,7},{1,0},{2,1},{3,2},{4,3},{5,4},{6,5},{7,6},{8,15},{9,8},{10,9... | collective-permute-start | bytes 786440 | tf_op jit(solution)/shard_map/ppermute | solution.py:26
